TPU v7x, 32 devices: a whole 2x2x4 slice. The times are simulated.
32 devices in a mesh: dp: 8 (over z, core), fsdp: 4 (over y, x).
Axes of the slice: x: 2, y: 2, z: 4, core: 2. Of those that a mesh axis runs over, the one named last changes fastest.
Arguments:
- normed: bfloat16 [12288, 4096], P(('dp', 'fsdp')), may hold values from -6 to 6
- queries: bfloat16 [12288, 2048], P(('dp', 'fsdp')), may hold values from -48 to 48
- key_rows: bfloat16 [12288, 512], P(('dp', 'fsdp')), may hold values from -6 to 6
- out_grad: bfloat16 [12288, 2048], P(('dp', 'fsdp')), may hold values from -6 to 6
- value_weight: bfloat16 [4096, 512], P('fsdp'), may hold values from -0.09375 to 0.09375
- doc_ids: int32 [32, 384], P(('dp', 'fsdp')), may hold values from 0 to 3, never falling along the last dimension, each value on 1 to 256 neighbouring positions
- send_to: int32 [32, 8], P(('dp', 'fsdp')), may hold values from 0 to 7, as said below
- take_from: int32 [32, 8], P(('dp', 'fsdp')), may hold values from 0 to 7, as said below
Outputs:
- query_grad: bfloat16 [12288, 2048], P(('dp', 'fsdp'))
- key_grad: bfloat16 [12288, 512], P(('dp', 'fsdp'))
- input_grad: bfloat16 [12288, 4096], P(('dp', 'fsdp'))
- weight_grad: float32 [4096, 512], P(('dp', 'fsdp'))
Inputs may be any that keep to these rules, and one draw needn't show every extreme that they name: `send_to`: entry b of a device's row names the dp index of the device, with the same fsdp index, that packs this device's rows b * 48 to (b + 1) * 48 - 1; the 8 entries of a row are distinct, and every device packs exactly 8 blocks. `take_from`: entry p of a device's row names the dp index of the device whose block, sent to this device by send_to, becomes this device's packed rows p * 48 to (p + 1) * 48 - 1; the entries of a row are distinct, so one device sends at most one block to another. `doc_ids`: along a device's 384 rows document numbers never fall; a document holds at most 256 rows, and one document in every draw holds exactly that many.
All inputs are finite; a program needn't handle non-finite values.
Results may differ from a plain program's by a relative error of at most 0.006.
Values may be sent and summed in bfloat16 or wider, within the bound.
A program may use at most 128 MiB of HBM per device.

v0:
```python
import jax
import jax.numpy as jnp
from jax import lax
from jax.sharding import PartitionSpec as P

HEADS = 16
KV_HEADS = 4
HEAD_DIM = 128
BLOCK_ROWS = 48


def to_slots(array, outgoing, blocks):
    shaped = array.reshape(blocks, BLOCK_ROWS, array.shape[1])
    return jnp.einsum("pb,bcw->pcw", outgoing, shaped, preferred_element_type=jnp.float32).astype(
        jnp.bfloat16
    )


def from_slots(array, incoming):
    picked = jnp.einsum("bs,scw->bcw", incoming, array, preferred_element_type=jnp.float32).astype(
        jnp.bfloat16
    )
    return picked.reshape(-1, array.shape[2])


def attend(packed_q, packed_k, packed_v, out_grad, doc_row):
    row_count = packed_q.shape[0]
    group_size = HEADS // KV_HEADS
    score_scale = HEAD_DIM ** (-0.5)
    query_heads = packed_q.reshape(row_count, KV_HEADS, group_size, HEAD_DIM)
    grad_heads = out_grad.reshape(row_count, KV_HEADS, group_size, HEAD_DIM)
    key_heads = packed_k.reshape(row_count, KV_HEADS, HEAD_DIM)
    value_heads = packed_v.reshape(row_count, KV_HEADS, HEAD_DIM)
    scores = (
        jnp.einsum("igxd,jgd->gxij", query_heads, key_heads, preferred_element_type=jnp.float32)
        * score_scale
    )
    positions = jnp.arange(row_count, dtype=jnp.int32)
    allowed = (doc_row[:, None] == doc_row[None, :]) & (positions[None, :] <= positions[:, None])
    masked = jnp.where(allowed, scores, -jnp.inf)
    row_peak = jnp.max(masked, axis=-1, keepdims=True)
    exponent = jnp.exp(masked - row_peak)
    attn_probs = exponent / jnp.sum(exponent, axis=-1, keepdims=True)
    probs_half = attn_probs.astype(jnp.bfloat16)
    attn_out = jnp.einsum(
        "gxij,jgd->igxd", probs_half, value_heads, preferred_element_type=jnp.float32
    )
    delta_rows = jnp.sum(grad_heads.astype(jnp.float32) * attn_out, axis=-1)
    prob_grad = jnp.einsum(
        "igxd,jgd->gxij", grad_heads, value_heads, preferred_element_type=jnp.float32
    )
    score_grad = (
        attn_probs * (prob_grad - jnp.transpose(delta_rows, (1, 2, 0))[..., None]) * score_scale
    ).astype(jnp.bfloat16)
    query_grad = jnp.einsum(
        "gxij,jgd->igxd", score_grad, key_heads, preferred_element_type=jnp.float32
    )
    key_grad = jnp.einsum(
        "gxij,igxd->jgd", score_grad, query_heads, preferred_element_type=jnp.float32
    )
    value_grad = jnp.einsum(
        "gxij,igxd->jgd", probs_half, grad_heads, preferred_element_type=jnp.float32
    )
    return (
        query_grad.astype(jnp.bfloat16).reshape(row_count, -1),
        key_grad.astype(jnp.bfloat16).reshape(row_count, -1),
        value_grad.astype(jnp.bfloat16).reshape(row_count, -1),
    )


def local(normed, queries, key_rows, out_grad, value_weight, doc_ids, send_to, take_from):
    dp_count = lax.axis_size("dp")
    fsdp_count = lax.axis_size("fsdp")
    row_count = normed.shape[0]
    blocks = row_count // BLOCK_ROWS
    grad_scale = (row_count * dp_count * fsdp_count) ** (-0.5)
    dp_lanes = jnp.arange(dp_count, dtype=jnp.int32)
    outgoing = (send_to[0][None, :] == dp_lanes[:, None]).astype(jnp.bfloat16)
    incoming = (take_from[0][:, None] == dp_lanes[None, :]).astype(jnp.bfloat16)
    columns = normed
    values = jnp.dot(
        columns,
        lax.all_gather(value_weight, "fsdp", axis=0, tiled=True),
        preferred_element_type=jnp.float32,
    ).astype(jnp.bfloat16)
    arrived = (
        lax.all_to_all(
            to_slots(queries, outgoing, blocks), "dp", split_axis=0, concat_axis=0, tiled=True
        ),
        lax.all_to_all(
            to_slots(key_rows, outgoing, blocks), "dp", split_axis=0, concat_axis=0, tiled=True
        ),
        lax.all_to_all(
            to_slots(values, outgoing, blocks), "dp", split_axis=0, concat_axis=0, tiled=True
        ),
    )
    packed_q = from_slots(arrived[0], incoming)
    packed_k = from_slots(arrived[1], incoming)
    packed_v = from_slots(arrived[2], incoming)
    query_grad, key_grad, value_grad = attend(packed_q, packed_k, packed_v, out_grad, doc_ids[0])
    input_grad = lax.dot_general(
        value_grad,
        lax.all_gather(value_weight, "fsdp", axis=0, tiled=True),
        (((1,), (1,)), ((), ())),
        preferred_element_type=jnp.float32,
    )
    input_grad = input_grad.astype(jnp.bfloat16)
    shaped = value_grad.reshape(blocks, BLOCK_ROWS, value_grad.shape[1])
    returning = jnp.einsum(
        "bs,bcw->scw", incoming, shaped, preferred_element_type=jnp.float32
    ).astype(jnp.bfloat16)
    landed = lax.all_to_all(returning, "dp", split_axis=0, concat_axis=0, tiled=True)
    pair_grad = (
        jnp.einsum("pb,pcw->bcw", outgoing, landed, preferred_element_type=jnp.float32)
        .astype(jnp.bfloat16)
        .reshape(row_count, -1)
    )
    columns = normed
    partial_grad = lax.psum_scatter(
        lax.dot_general(
            columns, pair_grad, (((0,), (0,)), ((), ())), preferred_element_type=jnp.float32
        )
        * grad_scale,
        "dp",
        scatter_dimension=0,
        tiled=True,
    )
    weight_grad = lax.psum_scatter(partial_grad, "fsdp", scatter_dimension=0, tiled=True)
    return (query_grad, key_grad, input_grad, weight_grad)


def solution(mesh):
    placed = (
        P(("dp", "fsdp"), None),
        P(("dp", "fsdp"), None),
        P(("dp", "fsdp"), None),
        P(("dp", "fsdp"), None),
        P("fsdp", None),
        P(("dp", "fsdp"), None),
        P(("dp", "fsdp"), None),
        P(("dp", "fsdp"), None),
    )
    return jax.shard_map(
        local,
        mesh=mesh,
        in_specs=placed,
        out_specs=(
            P(("dp", "fsdp"), None),
            P(("dp", "fsdp"), None),
            P(("dp", "fsdp"), None),
            P(("dp", "fsdp"), None),
        ),
        check_vma=False,
    )
```

profile of v0, /device:TPU:0, one launch (start us, length us, event | category | flops | bytes accessed | tf_op | source)
XLA Modules:
  0.0 257.6 jit_solution(7164919891725505377)
XLA Ops:
  10.5 6.3 %all-to-all-start = ((bf16[8,48,512]{2,1,0:T(8,128)(2,1)}), bf16[8,48,512]{2,1,0:T(8,128)(2,1)S(1)}, u32[]{:S(2)}, u32[]{:S(2)}) async-start(bf16[8,48,512]{2,1,0:T(8,128)(2,1)} %copy.46), calls=%async_computation | async-start | bytes 786432 | tf_op jit(solution)/shard_map/all_to_all | solution.py:90
  16.8 2.6 %convolution_convert_fusion.2 = bf16[8,48,2048]{2,0,1:T(8,128)(2,1)S(1)} fusion(bf16[8,48,2048]{2,1,0:T(8,128)(2,1)} %bitcast.104, s32[8]{0:T(128)} %bitcast.109), kind=kOutput, calls=%fused_computation.18 | convolution fusion | flops 13369408 | bytes 3145760 | tf_op jit(solution)/shard_map/pb,bcw->pcw/dot_general | solution.py:14
  21.4 7.9 %all-to-all-done = bf16[8,48,512]{2,1,0:T(8,128)(2,1)S(1)} async-done(((bf16[8,48,512]{2,1,0:T(8,128)(2,1)}), bf16[8,48,512]{2,1,0:T(8,128)(2,1)S(1)}, u32[]{:S(2)}, u32[]{:S(2)}) %all-to-all-start) | async-done | bytes 393248 | tf_op jit(solution)/shard_map/all_to_all | solution.py:90
  29.4 4.3 %all-to-all-start.1 = ((bf16[8,48,2048]{2,1,0:T(8,128)(2,1)}), bf16[8,48,2048]{2,1,0:T(8,128)(2,1)}, u32[]{:S(2)}, u32[]{:S(2)}) async-start(bf16[8,48,2048]{2,1,0:T(8,128)(2,1)} %copy.52), calls=%async_computation.1 | async-start | bytes 3145728 | tf_op jit(solution)/shard_map/all_to_all | solution.py:87
  34.6 2.6 %copy.64 = bf16[384,2048]{0,1:T(8,128)(2,1)} copy(bf16[384,2048]{1,0:T(8,128)(2,1)} %param.11) | data formatting | bytes 3145728 | tf_op args[3]
  40.6 30.9 %all-to-all-done.1 = bf16[8,48,2048]{2,1,0:T(8,128)(2,1)} async-done(((bf16[8,48,2048]{2,1,0:T(8,128)(2,1)}), bf16[8,48,2048]{2,1,0:T(8,128)(2,1)}, u32[]{:S(2)}, u32[]{:S(2)}) %all-to-all-start.1) | async-done | bytes 1572896 | tf_op jit(solution)/shard_map/all_to_all | solution.py:87
  71.5 2.5 convolution_convert_fusion.1
  76.0 3.8 %reshape_reshape.13 = bf16[384,4,4,128]{3,2,1,0:T(4,128)(2,1)} reshape(bf16[8,48,2048]{2,1,0:T(8,128)(2,1)} %copy.55) | data formatting | bytes 3145728 | tf_op jit(solution)/shard_map/reshape;reshape | solution.py:30
  79.8 3.9 %copy.71 = bf16[384,4,4,128]{0,3,2,1:T(8,128)(2,1)} copy(bf16[384,4,4,128]{3,2,1,0:T(4,128)(2,1)} %reshape_reshape.13) | data formatting | bytes 3145728 | tf_op jit(solution)/shard_map/reshape;reshape | solution.py:30
  83.8 8.7 %fusion.43 = (f32[4,4,384]{2,1,0:T(4,128)}, f32[4,4,384,384]{2,3,1,0:T(8,128)}) fusion(pred[384,384]{0,1:T(8,128)(4,1)} %fusion.16, bf16[384,4,128,1]{0,2,3,1:T(8,128)(2,1)S(1)} %copy.93, bf16[384,4,4,128]{0,3,2,1:T(8,128)(2,1)} %copy.71), kind=kOutput, calls=%fused_computation.56 | convolution fusion | flops 613417344 | bytes 11575296 | tf_op jit(solution)/shard_map/sub | solution.py:42
  92.5 4.8 %fusion.8 = bf16[4,4,384,384]{2,3,1,0:T(8,128)(2,1)S(1)} fusion(f32[4,4,384,384]{2,3,1,0:T(8,128)} %get-tuple-element.17, f32[4,4,384]{2,1,0:T(4,128)} %get-tuple-element.16), kind=kLoop, calls=%fused_computation.14 | loop fusion | flops 4718592 | bytes 14180352 | tf_op jit(solution)/shard_map/convert_element_type | solution.py:44
  104.9 14.9 %all_to_all.20 = bf16[8,48,512]{2,1,0:T(8,128)(2,1)S(1)} all-to-all(bf16[8,48,512]{2,1,0:T(8,128)(2,1)S(1)} %copy.76), channel_id=1, replica_groups=mesh['dp'=8,'fsdp'=4] {'dp'}, dimensions={0} | all-to-all | bytes 786432 | tf_op jit(solution)/shard_map/all_to_all | solution.py:112
  120.4 5.7 %multiply_bitcast_fusion = f32[4096,512]{0,1:T(8,128)} fusion(bf16[384,512]{1,0:T(8,128)(2,1)S(1)} %bitcast.98, bf16[384,4096]{1,0:T(8,128)(2,1)S(1)} %copy-done), kind=kOutput, calls=%fused_computation.7 | convolution fusion | flops 1612709888 | bytes 11927552 | tf_op jit(solution)/shard_map/dot_general | solution.py:120
  126.1 4.0 %convolution_convert_fusion.10 = bf16[384,512]{1,0:T(8,128)(2,1)S(1)} fusion(bf16[384,4096]{1,0:T(8,128)(2,1)S(1)} %copy-done, bf16[4096,512]{1,0:T(8,128)(2,1)} %all-gather.2.cloned.1.call-done), kind=kOutput, calls=%fused_computation.32 | convolution fusion | flops 1610809344 | bytes 7733248 | tf_op jit(solution)/shard_map/dot_general | solution.py:81
  131.4 3.5 %all-to-all-start.2 = ((bf16[8,48,512]{2,1,0:T(8,128)(2,1)}), bf16[8,48,512]{2,1,0:T(8,128)(2,1)S(1)}, u32[]{:S(2)}, u32[]{:S(2)}) async-start(bf16[8,48,512]{2,1,0:T(8,128)(2,1)} %copy.60), calls=%async_computation.2 | async-start | bytes 786432 | tf_op jit(solution)/shard_map/all_to_all | solution.py:93
  134.9 5.8 %convolution_convert_fusion = bf16[384,4096]{1,0:T(8,128)(2,1)} fusion(bf16[384,512]{0,1:T(8,128)(2,1)} %bitcast.100, bf16[4096,512]{1,0:T(8,128)(2,1)} %all-gather.2.cloned.1.call-done), kind=kOutput, calls=%fused_computation.9 | convolution fusion | flops 1612185600 | bytes 7733248 | tf_op jit(solution)/shard_map/dot_general | solution.py:101
  140.7 13.1 %all-to-all-done.2 = bf16[8,48,512]{2,1,0:T(8,128)(2,1)S(1)} async-done(((bf16[8,48,512]{2,1,0:T(8,128)(2,1)}), bf16[8,48,512]{2,1,0:T(8,128)(2,1)S(1)}, u32[]{:S(2)}, u32[]{:S(2)}) %all-to-all-start.2) | async-done | bytes 393248 | tf_op jit(solution)/shard_map/all_to_all | solution.py:93
  154.7 3.4 %fusion.9 = f32[384,4,4]{0,2,1:T(4,128)S(1)} fusion(bf16[384,4,4,128]{0,3,2,1:T(8,128)(2,1)S(1)} %bitcast.95, bf16[384,4,128,1]{0,2,3,1:T(8,128)(2,1)S(1)} %copy.91, bf16[4,4,384,384]{2,3,1,0:T(8,128)(2,1)} %copy-done.2), kind=kOutput, calls=%fused_computation.16 | convolution fusion | flops 606332928 | bytes 6709248 | tf_op jit(solution)/shard_map/gxij,jgd->igxd/dot_general | solution.py:45
  158.2 62.6 %reduce-scatter.3.cloned.1.call-done = f32[512,512]{0,1:T(8,128)} async-done(((f32[4096,512]{0,1:T(8,128)}), f32[512,512]{0,1:T(8,128)}) %reduce-scatter.3.cloned.1.call-update) | async-done | bytes 1048592 | tf_op jit(solution)/shard_map/reduce_scatter | solution.py:119
  220.9 4.8 %fusion.3 = bf16[4,4,384,384]{2,3,1,0:T(8,128)(2,1)S(1)} fusion(f32[4,4,384]{2,1,0:T(4,128)S(1)} %bitcast.107, f32[4,4,384,384]{2,3,1,0:T(8,128)} %get-tuple-element.17, f32[4,4,384]{2,1,0:T(4,128)S(1)} %copy-done.6, bf16[384,4,128,1]{0,2,3,1:T(8,128)(2,1)S(1)} %copy.91, bf16[384,4,4,128]{0,3,2,1:T(8,128)(2,1)S(1)} %bitcast.96), kind=kOutput, calls=%fused_computation.4 | convolution fusion | flops 615776256 | bytes 16171008 | tf_op jit(solution)/shard_map/igxd,jgd->gxij/dot_general | solution.py:49
  225.7 2.7 %convolution_convert_fusion.3 = bf16[4,128,4,384]{3,1,2,0:T(8,128)(2,1)} fusion(bf16[384,4,128,1]{0,2,3,1:T(8,128)(2,1)S(1)} %copy.93, bf16[4,4,384,384]{2,3,1,0:T(8,128)(2,1)S(1)} %fusion.3), kind=kOutput, calls=%fused_computation.19 | convolution fusion | flops 604766208 | bytes 6684672 | tf_op jit(solution)/shard_map/gxij,jgd->igxd/dot_general | solution.py:55
  228.4 2.7 %copy.79 = bf16[384,2048]{1,0:T(8,128)(2,1)} copy(bf16[384,2048]{0,1:T(8,128)(2,1)} %bitcast.97) | data formatting | bytes 3145728
  231.1 4.5 %fusion.12 = bf16[4,128,384]{2,1,0:T(8,128)(2,1)S(1)} fusion(bf16[384,4,4,128]{0,3,2,1:T(8,128)(2,1)} %copy.71, bf16[4,4,384,384]{2,3,1,0:T(8,128)(2,1)} %copy-done.3), kind=kOutput, calls=%fused_computation.24 | convolution fusion | flops 604176384 | bytes 6684672 | tf_op jit(solution)/shard_map/gxij,igxd->jgd/dot_general | solution.py:58
  236.6 11.8 %reduce-scatter.5.cloned.1.call-done = f32[128,512]{0,1:T(8,128)} async-done(((f32[512,512]{0,1:T(8,128)}), f32[128,512]{0,1:T(8,128)}) %reduce-scatter.5.cloned.1.call-update) | async-done | bytes 262160 | tf_op jit(solution)/shard_map/reduce_scatter | solution.py:128
  (52 shorter events, 23.8 us)
Async XLA Ops:
  8.0 112.3 %copy-start = (bf16[384,4096]{1,0:T(8,128)(2,1)S(1)}, bf16[384,4096]{1,0:T(8,128)(2,1)}, u32[]{:S(2)}) copy-start(bf16[384,4096]{1,0:T(8,128)(2,1)} %param.8) | copy-start | bytes 9437188
  10.5 18.9 %all-to-all-start = ((bf16[8,48,512]{2,1,0:T(8,128)(2,1)}), bf16[8,48,512]{2,1,0:T(8,128)(2,1)S(1)}, u32[]{:S(2)}, u32[]{:S(2)}) async-start(bf16[8,48,512]{2,1,0:T(8,128)(2,1)} %copy.46), calls=%async_computation | async-start | bytes 786432 | tf_op jit(solution)/shard_map/all_to_all | solution.py:90
  21.4 15.8 %copy-start.9 = (s32[1,384]{1,0:T(1,128)S(1)}, s32[1,384]{1,0:T(1,128)}, u32[]{:S(2)}) copy-start(s32[1,384]{1,0:T(1,128)} %param.13) | copy-start | bytes 4612
  21.4 16.6 %copy-start.8 = (s32[1,8]{1,0:T(1,128)S(1)}, s32[1,8]{1,0:T(1,128)}, u32[]{:S(2)}) copy-start(s32[1,8]{1,0:T(1,128)} %param.15) | copy-start | bytes 100
  29.4 42.1 %all-to-all-start.1 = ((bf16[8,48,2048]{2,1,0:T(8,128)(2,1)}), bf16[8,48,2048]{2,1,0:T(8,128)(2,1)}, u32[]{:S(2)}, u32[]{:S(2)}) async-start(bf16[8,48,2048]{2,1,0:T(8,128)(2,1)} %copy.52), calls=%async_computation.1 | async-start | bytes 3145728 | tf_op jit(solution)/shard_map/all_to_all | solution.py:87
  33.6 92.4 %all-gather.2.cloned.1.call-start = ((), (), s32[]{:S(2)}) async-start(), calls=%async_computation.6 | async-start | bytes 5242880 | tf_op jit(solution)/shard_map/all_gather | solution.py:83
  34.4 186.4 %reduce-scatter.3.cloned.1.call-start = ((), (), s32[]{:S(2)}) async-start(), calls=%async_computation.7 | async-start | bytes 9437184 | tf_op jit(solution)/shard_map/reduce_scatter | solution.py:119
  92.5 4.8 %copy-start.4 = (bf16[384,2048]{0,1:T(8,128)(2,1)S(1)}, bf16[384,2048]{0,1:T(8,128)(2,1)}, u32[]{:S(2)}) copy-start(bf16[384,2048]{0,1:T(8,128)(2,1)} %copy.64) | copy-start | bytes 4718596
  97.3 2.3 copy-start.2
  99.6 20.2 %copy-start.7 = (s32[1,8]{1,0:T(1,128)S(1)}, s32[1,8]{1,0:T(1,128)}, u32[]{:S(2)}) copy-start(s32[1,8]{1,0:T(1,128)} %param.14) | copy-start | bytes 100
  131.4 22.5 %all-to-all-start.2 = ((bf16[8,48,512]{2,1,0:T(8,128)(2,1)}), bf16[8,48,512]{2,1,0:T(8,128)(2,1)S(1)}, u32[]{:S(2)}, u32[]{:S(2)}) async-start(bf16[8,48,512]{2,1,0:T(8,128)(2,1)} %copy.60), calls=%async_computation.2 | async-start | bytes 786432 | tf_op jit(solution)/shard_map/all_to_all | solution.py:93
  134.8 113.5 %reduce-scatter.5.cloned.1.call-start = ((), (), s32[]{:S(2)}) async-start(), calls=%async_computation.8 | async-start | bytes 1310720 | tf_op jit(solution)/shard_map/reduce_scatter | solution.py:128
  140.7 14.0 %copy-start.5 = (bf16[384,2048]{0,1:T(8,128)(2,1)S(1)}, bf16[384,2048]{0,1:T(8,128)(2,1)}, u32[]{:S(2)}) copy-start(bf16[384,2048]{0,1:T(8,128)(2,1)} %copy.64) | copy-start | bytes 4718596
  154.7 66.1 %copy-start.6 = (f32[4,4,384]{2,1,0:T(4,128)S(1)}, f32[4,4,384]{2,1,0:T(4,128)}, u32[]{:S(2)}) copy-start(f32[4,4,384]{2,1,0:T(4,128)} %get-tuple-element.16) | copy-start | bytes 73732
  225.7 2.7 %copy-start.3 = (bf16[4,4,384,384]{2,3,1,0:T(8,128)(2,1)}, bf16[4,4,384,384]{2,3,1,0:T(8,128)(2,1)S(1)}, u32[]{:S(2)}) copy-start(bf16[4,4,384,384]{2,3,1,0:T(8,128)(2,1)S(1)} %fusion.3) | copy-start | bytes 14155780
  228.4 21.8 %copy-start.1 = (bf16[384,4096]{1,0:T(8,128)(2,1)S(1)}, bf16[384,4096]{1,0:T(8,128)(2,1)}, u32[]{:S(2)}) copy-start(bf16[384,4096]{1,0:T(8,128)(2,1)} %param.8) | copy-start | bytes 9437188
Sparse Core Ops, SparseCore 0:
  36.3 54.0 all-gather.1
  221.0 27.3 reduce-scatter.4
Sparse Core Ops, SparseCore 1:
  126.1 94.6 reduce-scatter.2
where the time goes:
time: 258 us
  waiting for transfers between devices  127 us (49%)
  matrix products  51.5 us (20%)
  local copies, waits for them, and re-layouts  28.4 us (11%)
  between operations  15.7 us (6%)
  blocking collectives  14.9 us (6%)
  starting transfers between devices  14.4 us (6%)
  other arithmetic  5.64 us (2%)
    reduce_scatter x1, waiting for transfers between devices, local(): lax.psum_scatter(lax.dot_general(columns, pair_grad, (((0,), (0,)), ((),...  62.6 us
    all_to_all x1, waiting for transfers between devices, local(): lax.all_to_all(to_slots(queries, outgoing, blocks), 'dp', split_axis=0, c...  30.9 us
    all_to_all x1, blocking collectives, local(): lax.all_to_all(returning, 'dp', split_axis=0, concat_axis=0, tiled=True)  14.9 us
    all_to_all x1, waiting for transfers between devices, local(): lax.all_to_all(to_slots(values, outgoing, blocks), 'dp', split_axis=0, co...  13.1 us
    reduce_scatter x1, waiting for transfers between devices, local(): lax.psum_scatter(partial_grad, 'fsdp', scatter_dimension=0, tiled=True)  11.8 us
    sub x1, matrix products, attend(): exponent = jnp.exp(masked - row_peak)  8.7 us
    unnamed x24, local copies, waits for them, and re-layouts  8.08 us
    all_to_all x1, waiting for transfers between devices, local(): lax.all_to_all(to_slots(key_rows, outgoing, blocks), 'dp', split_axis=0,...  7.91 us
  transfers between devices with their start and end apart: 6, of which 5 were waited for; matrix products, arithmetic and copies ran while one was open for 32% of the time, Pallas kernels for 0%

commit v1 on v0

v1 whole, which is shorter than its diff:
```python
import functools

import jax
import jax.numpy as jnp
from jax import lax
from jax.experimental import pallas as pl
from jax.experimental.pallas import tpu as pltpu
from jax.sharding import PartitionSpec as P

HEADS = 16
KV_HEADS = 4
HEAD_DIM = 128
GROUP = HEADS // KV_HEADS
GROUP_COLS = GROUP * HEAD_DIM
KV_COLS = KV_HEADS * HEAD_DIM
BLOCK_ROWS = 48
TILE = 128
HALF_COLS = KV_COLS // 2
MASKED = -1e30
MESH = pl.DeviceIdType.MESH
CH_K, CH_V, CH_Q, CH_G = 0, 1, 2, 2 + KV_HEADS
NT = (((1,), (1,)), ((), ()))
TN = (((0,), (0,)), ((), ()))


def kernel(
    n_dp, n_f, grad_scale,
    normed, queries, keys, out_grad, weight, doc_row, send_to, take_from, send_block, take_block,
    query_grad, key_grad, input_grad, weight_grad,
    tx, rx, gtx, grx, whole_w, values_f32, values, packed_q, packed_k, packed_v,
    normed_t, bias, dk_acc, dv_acc, value_grad, home, pair_tx, pair_rx, pair_sum,
    f_rx, z_tx, z_rx,
    a_send, a_recv, w_send, w_recv, ws_send, ws_recv, p_send, p_recv, f_send, f_recv,
    z_send, z_recv,
):
    rows, width = normed.shape
    blocks = rows // BLOCK_ROWS
    n_z = n_dp // 2
    shard = width // n_f
    half = shard // 2
    dest_rows = width // n_dp
    piece = dest_rows // n_f
    d = lax.axis_index("dp")
    f = lax.axis_index("fsdp")
    core = lax.rem(d, 2)
    z = lax.div(d, 2)
    sibling = d + 1 - 2 * core

    def dp_peer(i):
        return lax.rem(d + i, n_dp)

    def f_peer(i):
        return lax.rem(f + i, n_f)

    barrier = pltpu.get_barrier_semaphore()

    def greet_dp(i, _):
        pl.semaphore_signal(barrier, inc=1, device_id={"dp": dp_peer(i)}, device_id_type=MESH)
        return 0

    def greet_f(i, _):
        pl.semaphore_signal(barrier, inc=1, device_id={"fsdp": f_peer(i)}, device_id_type=MESH)
        return 0

    lax.fori_loop(1, n_dp, greet_dp, 0)
    lax.fori_loop(1, n_f, greet_f, 0)

    def to_slots(source, column, cols, table, out, own):
        def body(p, _):
            out[p] = source[table[0, p], :, column : column + cols]
            return 0

        lax.fori_loop(0, n_dp, body, 0)
        own[d] = out[d]

    def from_slots(landed, table, out, column, cols):
        for p in range(blocks):
            out[p * BLOCK_ROWS : (p + 1) * BLOCK_ROWS, column : column + cols] = landed[table[0, p]]

    def exchange(channel, out, landed, i):
        to = dp_peer(i)
        return pltpu.make_async_remote_copy(
            src_ref=out.at[to],
            dst_ref=landed.at[d],
            send_sem=a_send.at[channel, to],
            recv_sem=a_recv.at[channel, d],
            device_id={"dp": to},
            device_id_type=MESH,
        )

    def arrival(channel, out, landed, i):
        source = dp_peer(i)
        return pltpu.make_async_remote_copy(
            src_ref=out.at[source],
            dst_ref=landed.at[source],
            send_sem=a_send.at[channel, source],
            recv_sem=a_recv.at[channel, source],
            device_id={"dp": source},
            device_id_type=MESH,
        )

    def each(low, high, act):
        def body(i, _):
            act(i)
            return 0

        lax.fori_loop(low, high, body, 0)

    def send_all(channel, out, landed):
        each(1, n_dp, lambda i: exchange(channel, out, landed, i).start())

    def recv_all(channel, out, landed):
        each(1, n_dp, lambda i: arrival(channel, out, landed, i).wait_recv())

    def w_copy(i):
        to = f_peer(i)
        return pltpu.make_async_remote_copy(
            src_ref=weight.at[pl.ds(pl.multiple_of(core * half, 16), half)],
            dst_ref=whole_w.at[f, core],
            send_sem=w_send.at[to],
            recv_sem=w_recv.at[f],
            device_id={"fsdp": to},
            device_id_type=MESH,
        )

    def w_arrival(i):
        source = f_peer(i)
        return pltpu.make_async_remote_copy(
            src_ref=weight.at[pl.ds(pl.multiple_of(core * half, 16), half)],
            dst_ref=whole_w.at[source, core],
            send_sem=w_send.at[source],
            recv_sem=w_recv.at[source],
            device_id={"fsdp": source},
            device_id_type=MESH,
        )

    def w_forward(i):
        source = f_peer(i)
        return pltpu.make_async_remote_copy(
            src_ref=whole_w.at[source, core],
            dst_ref=whole_w.at[source, core],
            send_sem=ws_send.at[source],
            recv_sem=ws_recv.at[source],
            device_id={"dp": sibling},
            device_id_type=MESH,
        )

    def w_forwarded(i):
        source = f_peer(i)
        return pltpu.make_async_remote_copy(
            src_ref=whole_w.at[source, 1 - core],
            dst_ref=whole_w.at[source, 1 - core],
            send_sem=ws_send.at[source],
            recv_sem=ws_recv.at[source],
            device_id={"dp": sibling},
            device_id_type=MESH,
        )

    to_slots(keys, 0, KV_COLS, send_block, tx[CH_K], rx[CH_K])
    to_slots(queries, 0, GROUP_COLS, send_block, tx[CH_Q], rx[CH_Q])
    pl.semaphore_wait(barrier, n_dp + n_f - 2)

    each(1, n_f, lambda i: w_copy(i).start())
    send_all(CH_K, tx[CH_K], rx[CH_K])
    send_all(CH_Q, tx[CH_Q], rx[CH_Q])
    for g in range(1, KV_HEADS):
        to_slots(queries, g * GROUP_COLS, GROUP_COLS, send_block, tx[CH_Q + g], rx[CH_Q + g])
        if g == 1:
            send_all(CH_Q + g, tx[CH_Q + g], rx[CH_Q + g])

    whole_w[f, 0] = weight[:half]
    whole_w[f, 1] = weight[half:]

    def transpose(c, _):
        at = pl.multiple_of(c * 256, 256)
        normed_t[pl.ds(at, 256), :] = normed[:, pl.ds(at, 256)].T
        return 0

    lax.fori_loop(0, width // 256, transpose, 0)

    docs_across = jnp.broadcast_to(doc_row[...], (TILE, rows))
    docs_down = docs_across.T
    for j in range(rows // TILE):
        same = docs_down == jnp.broadcast_to(doc_row[:, j * TILE : (j + 1) * TILE], (rows, TILE))
        i_at = lax.broadcasted_iota(jnp.int32, (rows, TILE), 0)
        j_at = lax.broadcasted_iota(jnp.int32, (rows, TILE), 1) + j * TILE
        bias[:, j * TILE : (j + 1) * TILE] = jnp.where(same & (j_at <= i_at), 0.0, MASKED)

    def add_values(i, first):
        at = f_peer(i)
        cols = normed[:, pl.ds(pl.multiple_of(at * shard, 128), shard)]
        term = jnp.dot(
            cols, whole_w[at].reshape(shard, KV_COLS), preferred_element_type=jnp.float32
        )
        values_f32[...] = term if first else values_f32[...] + term

    add_values(0, True)

    def forward(i):
        w_arrival(i).wait_recv()
        w_forward(i).start()

    each(1, n_f, forward)

    def later_values(i):
        w_forwarded(i).wait_recv()
        add_values(i, False)

    each(1, n_f, later_values)
    values[...] = values_f32[...].astype(jnp.bfloat16).reshape(values.shape)
    to_slots(values, 0, KV_COLS, send_block, tx[CH_V], rx[CH_V])
    send_all(CH_V, tx[CH_V], rx[CH_V])
    for g in range(2, KV_HEADS):
        send_all(CH_Q + g, tx[CH_Q + g], rx[CH_Q + g])

    recv_all(CH_K, tx[CH_K], rx[CH_K])
    from_slots(rx[CH_K], take_from, packed_k, 0, KV_COLS)

    scale = HEAD_DIM ** (-0.5)

    def attend(g):
        recv_all(CH_Q + g, tx[CH_Q + g], rx[CH_Q + g])
        from_slots(rx[CH_Q + g], take_from, packed_q, g * GROUP_COLS, GROUP_COLS)
        if g == 0:
            recv_all(CH_V, tx[CH_V], rx[CH_V])
            from_slots(rx[CH_V], take_from, packed_v, 0, KV_COLS)
        kv = slice(g * HEAD_DIM, (g + 1) * HEAD_DIM)
        for t in reversed(range(rows // TILE)):
            span = (t + 1) * TILE
            here = slice(t * TILE, span)
            heads = [
                slice(g * GROUP_COLS + x * HEAD_DIM, g * GROUP_COLS + (x + 1) * HEAD_DIM)
                for x in range(GROUP)
            ]
            q = jnp.concatenate([packed_q[here, h] for h in heads], axis=0)
            og = jnp.concatenate([out_grad[here, h] for h in heads], axis=0)
            k = packed_k[:span, kv]
            v = packed_v[:span, kv]
            s = lax.dot_general(q, k, NT, preferred_element_type=jnp.float32) * scale
            s = (s.reshape(GROUP, TILE, span) + bias[here, :span][None]).reshape(GROUP * TILE, span)
            peak = jnp.max(s, axis=-1, keepdims=True)
            e = jnp.exp(s - peak)
            p = e * (1.0 / jnp.sum(e, axis=-1, keepdims=True))
            ph = p.astype(jnp.bfloat16)
            pg = lax.dot_general(og, v, NT, preferred_element_type=jnp.float32)
            delta = jnp.sum(ph.astype(jnp.float32) * pg, axis=-1, keepdims=True)
            ds = (p * (pg - delta) * scale).astype(jnp.bfloat16)
            dq = jnp.dot(ds, k, preferred_element_type=jnp.float32).astype(jnp.bfloat16)
            for x, h in enumerate(heads):
                query_grad[here, h] = dq[x * TILE : (x + 1) * TILE]
            dk = lax.dot_general(ds, q, TN, preferred_element_type=jnp.float32)
            dv = lax.dot_general(ph, og, TN, preferred_element_type=jnp.float32)
            if span == rows:
                dk_acc[...] = dk
                dv_acc[...] = dv
            else:
                dk_acc[:span] += dk
                dv_acc[:span] += dv
        key_grad[:, kv] = dk_acc[...].astype(jnp.bfloat16)
        value_grad[:, :, kv] = dv_acc[...].astype(jnp.bfloat16).reshape(blocks, BLOCK_ROWS, HEAD_DIM)

    def return_values(h):
        to_slots(value_grad, h * HALF_COLS, HALF_COLS, take_block, gtx[h], grx[h])
        send_all(CH_G + h, gtx[h], grx[h])

    def pair_copy(h):
        return pltpu.make_async_remote_copy(
            src_ref=pair_tx.at[h],
            dst_ref=pair_rx.at[h],
            send_sem=p_send.at[h],
            recv_sem=p_recv.at[h],
            device_id={"dp": sibling},
            device_id_type=MESH,
        )

    def product(h, zz, which):
        at = pl.multiple_of((zz * 2 + which) * dest_rows, 128)
        return jnp.dot(
            normed_t[pl.ds(at, dest_rows), :], home[h], preferred_element_type=jnp.float32
        )

    def weight_terms(h):
        recv_all(CH_G + h, gtx[h], grx[h])
        for b in range(blocks):
            home[h, b * BLOCK_ROWS : (b + 1) * BLOCK_ROWS, :] = grx[h][send_to[0, b]]

        def other(zz):
            pair_tx[h, zz] = product(h, zz, 1 - core).astype(jnp.bfloat16)

        each(0, n_z, other)
        pair_copy(h).start()

    def f_copy(h, i):
        to = f_peer(i)
        return pltpu.make_async_remote_copy(
            src_ref=pair_sum.at[h, :, pl.ds(pl.multiple_of(to * piece, 16), piece)],
            dst_ref=f_rx.at[h, f],
            send_sem=f_send.at[h, to],
            recv_sem=f_recv.at[h, f],
            device_id={"fsdp": to},
            device_id_type=MESH,
        )

    def f_arrival(h, i):
        source = f_peer(i)
        return pltpu.make_async_remote_copy(
            src_ref=pair_sum.at[h, :, pl.ds(pl.multiple_of(source * piece, 16), piece)],
            dst_ref=f_rx.at[h, source],
            send_sem=f_send.at[h, source],
            recv_sem=f_recv.at[h, source],
            device_id={"fsdp": source},
            device_id_type=MESH,
        )

    def weight_pairs(h):
        pair_copy(h).wait_recv()

        def own(zz):
            total = product(h, zz, core) + pair_rx[h, zz].astype(jnp.float32)
            pair_sum[h, zz] = total.astype(jnp.bfloat16)

        each(0, n_z, own)
        each(1, n_f, lambda i: f_copy(h, i).start())

    def z_peer(i):
        return lax.rem(z + i, n_z)

    def z_copy(h, i):
        to = z_peer(i)
        return pltpu.make_async_remote_copy(
            src_ref=z_tx.at[h, to],
            dst_ref=z_rx.at[h, z],
            send_sem=z_send.at[h, to],
            recv_sem=z_recv.at[h, z],
            device_id={"dp": to * 2 + core},
            device_id_type=MESH,
        )

    def z_arrival(h, i):
        source = z_peer(i)
        return pltpu.make_async_remote_copy(
            src_ref=z_tx.at[h, source],
            dst_ref=z_rx.at[h, source],
            send_sem=z_send.at[h, source],
            recv_sem=z_recv.at[h, source],
            device_id={"dp": source * 2 + core},
            device_id_type=MESH,
        )

    def weight_squares(h):
        each(1, n_f, lambda i: f_arrival(h, i).wait_recv())
        mine = pl.multiple_of(f * piece, 16)

        def total(zz):
            acc = pair_sum[h, zz, pl.ds(mine, piece), :].astype(jnp.float32)
            for i in range(1, n_f):
                acc = acc + f_rx[h, f_peer(i), zz].astype(jnp.float32)
            z_tx[h, zz] = acc.astype(jnp.bfloat16)

        each(0, n_z, total)
        each(1, n_z, lambda i: z_copy(h, i).start())

    def weight_lines(h):
        each(1, n_z, lambda i: z_arrival(h, i).wait_recv())
        acc = z_tx[h, z].astype(jnp.float32)
        for i in range(1, n_z):
            acc = acc + z_rx[h, z_peer(i)].astype(jnp.float32)
        weight_grad[:, h * HALF_COLS : (h + 1) * HALF_COLS] = acc * grad_scale

    attend(0)
    attend(1)
    return_values(0)
    attend(2)
    weight_terms(0)
    attend(3)
    return_values(1)
    weight_pairs(0)

    def input_cols(at):
        w = whole_w[at].reshape(shard, KV_COLS)
        x = lax.dot_general(value_grad[...].reshape(rows, KV_COLS), w, NT, preferred_element_type=jnp.float32)
        input_grad[:, pl.ds(pl.multiple_of(at * shard, 128), shard)] = x.astype(jnp.bfloat16)

    weight_terms(1)
    each(0, n_f // 2, input_cols)
    weight_pairs(1)
    weight_squares(0)
    each(n_f // 2, n_f, input_cols)
    weight_squares(1)
    weight_lines(0)
    weight_lines(1)

    each(1, n_f, lambda i: w_copy(i).wait_send())
    each(1, n_f, lambda i: w_forward(i).wait_send())
    for channel in range(CH_G):
        each(1, n_dp, lambda i: exchange(channel, tx[channel], rx[channel], i).wait_send())
    for h in range(2):
        each(1, n_dp, lambda i: exchange(CH_G + h, gtx[h], grx[h], i).wait_send())
        pair_copy(h).wait_send()
        each(1, n_f, lambda i: f_copy(h, i).wait_send())
        each(1, n_z, lambda i: z_copy(h, i).wait_send())


def local(normed, queries, key_rows, out_grad, value_weight, doc_ids, send_to, take_from):
    n_dp = lax.axis_size("dp")
    n_f = lax.axis_size("fsdp")
    rows, width = normed.shape
    n_z = n_dp // 2
    shard = width // n_f
    dest_rows = width // n_dp
    piece = dest_rows // n_f
    half = jnp.bfloat16
    vmem = pl.BlockSpec(memory_space=pltpu.VMEM)
    smem = pl.BlockSpec(memory_space=pltpu.SMEM)
    dma = pltpu.SemaphoreType.DMA
    slots = [pltpu.VMEM((n_dp, BLOCK_ROWS, KV_COLS), half) for _ in range(CH_G)]
    half_slots = [pltpu.VMEM((n_dp, BLOCK_ROWS, HALF_COLS), half) for _ in range(2)]
    blocks = rows // BLOCK_ROWS
    lanes = jnp.arange(n_dp, dtype=jnp.int32)
    order = jnp.arange(blocks, dtype=jnp.int32)

    def inverse(table):
        return jnp.sum(
            jnp.where(table[:, :, None] == lanes, order[None, :, None], 0), axis=1, dtype=jnp.int32
        )

    return pl.pallas_call(
        functools.partial(kernel, n_dp, n_f, (rows * n_dp * n_f) ** (-0.5)),
        out_shape=(
            jax.ShapeDtypeStruct(queries.shape, half),
            jax.ShapeDtypeStruct(key_rows.shape, half),
            jax.ShapeDtypeStruct(normed.shape, half),
            jax.ShapeDtypeStruct((piece, KV_COLS), jnp.float32),
        ),
        in_specs=[vmem] * 6 + [smem] * 4,
        out_specs=(vmem,) * 4,
        scratch_shapes=[
            list(slots), list(slots), list(half_slots), list(half_slots),
            pltpu.VMEM((n_f, 2, shard // 2, KV_COLS), half),
            pltpu.VMEM((rows, KV_COLS), jnp.float32),
            pltpu.VMEM((rows // BLOCK_ROWS, BLOCK_ROWS, KV_COLS), half),
            pltpu.VMEM(queries.shape, half),
            pltpu.VMEM(key_rows.shape, half),
            pltpu.VMEM(key_rows.shape, half),
            pltpu.VMEM((width, rows), half),
            pltpu.VMEM((rows, rows), jnp.float32),
            pltpu.VMEM((rows, HEAD_DIM), jnp.float32),
            pltpu.VMEM((rows, HEAD_DIM), jnp.float32),
            pltpu.VMEM((rows // BLOCK_ROWS, BLOCK_ROWS, KV_COLS), half),
            pltpu.VMEM((2, rows, HALF_COLS), half),
            pltpu.VMEM((2, n_z, dest_rows, HALF_COLS), half),
            pltpu.VMEM((2, n_z, dest_rows, HALF_COLS), half),
            pltpu.VMEM((2, n_z, dest_rows, HALF_COLS), half),
            pltpu.VMEM((2, n_f, n_z, piece, HALF_COLS), half),
            pltpu.VMEM((2, n_z, piece, HALF_COLS), half),
            pltpu.VMEM((2, n_z, piece, HALF_COLS), half),
            dma((CH_G + 2, n_dp)), dma((CH_G + 2, n_dp)),
            dma((n_f,)), dma((n_f,)), dma((n_f,)), dma((n_f,)),
            dma((2,)), dma((2,)), dma((2, n_f)), dma((2, n_f)), dma((2, n_z)), dma((2, n_z)),
        ],
        compiler_params=pltpu.CompilerParams(
            collective_id=0, has_side_effects=True, vmem_limit_bytes=56 * 1024 * 1024
        ),
        cost_estimate=pl.CostEstimate(
            flops=10_000_000_000, bytes_accessed=16_000_000, transcendentals=2_400_000
        ),
        name="packed_backward",
    )(
        normed,
        queries.reshape(blocks, BLOCK_ROWS, queries.shape[1]),
        key_rows.reshape(blocks, BLOCK_ROWS, key_rows.shape[1]),
        out_grad, value_weight, doc_ids, send_to, take_from,
        inverse(send_to), inverse(take_from),
    )


def solution(mesh):
    rows = P(("dp", "fsdp"), None)
    return jax.shard_map(
        local,
        mesh=mesh,
        in_specs=(rows, rows, rows, rows, P("fsdp", None), rows, rows, rows),
        out_specs=(rows, rows, rows, rows),
        check_vma=False,
    )
```

time: 258 us -> 119 us (0.46)
  waiting for transfers between devices: 127 us -> 0 us
  Pallas kernels: 0 us -> 108 us
  matrix products: 51.5 us -> 0 us
  local copies, waits for them, and re-layouts: 28.4 us -> 7.02 us
  between operations: 15.7 us -> 0.65 us
  blocking collectives: 14.9 us -> 0 us
  starting transfers between devices: 14.4 us -> 0 us
  other arithmetic: 5.64 us -> 2.5 us
    pallas_call x0 -> x1, Pallas kernels: none -> 108 us  [local(): pl.pallas_call(functools.partial(kernel, n_dp, n_f, (rows * n_dp * n_f) *...]
    reduce_scatter x2 -> x0, waiting for transfers between devices: 74.4 us -> none  [the longest x1 62.6 us: local(): lax.psum_scatter(lax.dot_general(columns, pair_grad, (((0,), (0,)), ((),...]
    all_to_all x3 -> x0, waiting for transfers between devices: 51.9 us -> none  [the longest x1 30.9 us: local(): lax.all_to_all(to_slots(queries, outgoing, blocks), 'dp', split_axis=0, c...]
    dot_general x16 -> x0, matrix products: 42.8 us -> none  [the longest x1 5.84 us: local(): lax.dot_general(value_grad, lax.all_gather(value_weight, 'fsdp', axis=0,...]
    all_to_all x1 -> x0, blocking collectives: 14.9 us -> none  [local(): lax.all_to_all(returning, 'dp', split_axis=0, concat_axis=0, tiled=True)]
    all_to_all x3 -> x0, starting transfers between devices: 14.1 us -> none  [the longest x1 6.33 us: local(): lax.all_to_all(to_slots(key_rows, outgoing, blocks), 'dp', split_axis=0,...]
    another operation x7 -> x0, local copies, waits for them, and re-layouts: 12.1 us -> none  [the longest x2 7.73 us: attend(): query_heads = packed_q.reshape(row_count, KV_HEADS, group_size, HEAD_DIM)]
    sub x1 -> x0, matrix products: 8.7 us -> none  [attend(): exponent = jnp.exp(masked - row_peak)]
  transfers between devices with their start and end apart: 6 -> 0, of which waited for: 5 -> 0; matrix products, arithmetic and copies ran while one was open for 32% -> 0% of each run, Pallas kernels for 0% -> 0%
where the time goes in v1:
time: 119 us
  Pallas kernels  108 us (91%)
  local copies, waits for them, and re-layouts  7.02 us (6%)
  other arithmetic  2.5 us (2%)
    pallas_call x1, Pallas kernels, local(): pl.pallas_call(functools.partial(kernel, n_dp, n_f, (rows * n_dp * n_f) *...  108 us
    unnamed x8, local copies, waits for them, and re-layouts  7.02 us
    reduce_sum x2, other arithmetic, inverse(): jnp.sum(jnp.where(table[:, :, None] == lanes, order[None, :, None], 0), a...  2.5 us

profile of v1, /device:TPU:0, one launch (start us, length us, event | category | flops | bytes accessed | tf_op | source)
XLA Modules:
  0.0 118.5 jit_solution(5472457168470588317)
XLA Ops:
  0.6 1.2 %select_reduce_fusion = s32[8]{0:T(128)} fusion(s32[8]{0:T(128)} %bitcast.9), kind=kLoop, calls=%fused_computation | loop fusion | flops 184 | bytes 64 | tf_op jit(solution)/shard_map/reduce_sum | solution.py:423
  1.9 1.2 %select_reduce_fusion.1 = s32[8]{0:T(128)} fusion(s32[8]{0:T(128)} %bitcast.8), kind=kLoop, calls=%fused_computation.2 | loop fusion | flops 184 | bytes 64 | tf_op jit(solution)/shard_map/reduce_sum | solution.py:423
  3.1 108.4 %packed_backward.1 = (bf16[384,2048]{1,0:T(8,128)(2,1)}, bf16[384,512]{1,0:T(8,128)(2,1)}, bf16[384,4096]{1,0:T(8,128)(2,1)}, f32[128,512]{1,0:T(8,128)}) custom-call(bf16[384,4096]{1,0:T(8,128)(2,1)} %normed.1, bf16[8,48,2048]{2,1,0:T(8,128)(2,1)} %bitcast.6, bf16[8,48,512]{2,1,0:T(8,128)(2,1)} %bitcast.7, bf16[384,2048]{1,0:T(8,128)(2,1)} %out_grad.1, ...), custom_call_target="tpu_custom_call" | custom-call | flops 10000000000 | bytes 16000000 | tf_op jit(solution)/shard_map/packed_backward/pallas_call | solution.py:427
  111.5 0.0 copy-start
  111.5 2.9 %copy.16 = bf16[384,2048]{1,0:T(8,128)(2,1)} copy(bf16[384,2048]{1,0:T(8,128)(2,1)} %get-tuple-element.8) | data formatting | bytes 3145728
  114.4 1.8 %copy.17 = bf16[384,512]{1,0:T(8,128)(2,1)} copy(bf16[384,512]{1,0:T(8,128)(2,1)} %get-tuple-element.9) | data formatting | bytes 786432
  116.2 0.0 copy-done
  116.2 0.0 copy-start.1
  116.2 1.7 %copy.18 = bf16[384,4096]{1,0:T(8,128)(2,1)} copy(bf16[384,4096]{1,0:T(8,128)(2,1)S(1)} %copy-done) | data formatting | bytes 6291456
  117.8 0.0 copy-done.1
  117.8 0.7 copy.19
Async XLA Ops:
  111.5 4.7 %copy-start = (bf16[384,4096]{1,0:T(8,128)(2,1)S(1)}, bf16[384,4096]{1,0:T(8,128)(2,1)}, u32[]{:S(2)}) copy-start(bf16[384,4096]{1,0:T(8,128)(2,1)} %get-tuple-element.10) | copy-start | bytes 9437188
  116.2 1.7 %copy-start.1 = (f32[128,512]{1,0:T(8,128)S(1)}, f32[128,512]{1,0:T(8,128)}, u32[]{:S(2)}) copy-start(f32[128,512]{1,0:T(8,128)} %get-tuple-element.11) | copy-start | bytes 786436

commit v2 on v1

--- a/solution.py
+++ b/solution.py
@@ -28,7 +28,7 @@
     normed, queries, keys, out_grad, weight, doc_row, send_to, take_from, send_block, take_block,
     query_grad, key_grad, input_grad, weight_grad,
     tx, rx, gtx, grx, whole_w, values_f32, values, packed_q, packed_k, packed_v,
-    normed_t, bias, dk_acc, dv_acc, value_grad, home, pair_tx, pair_rx, pair_sum,
+    normed_t, bias, dk_acc, dv_acc, probs, value_grad, home, pair_tx, pair_rx, pair_sum,
     f_rx, z_tx, z_rx,
     a_send, a_recv, w_send, w_recv, ws_send, ws_recv, p_send, p_recv, f_send, f_recv,
     z_send, z_recv,
@@ -165,8 +165,7 @@
     send_all(CH_Q, tx[CH_Q], rx[CH_Q])
     for g in range(1, KV_HEADS):
         to_slots(queries, g * GROUP_COLS, GROUP_COLS, send_block, tx[CH_Q + g], rx[CH_Q + g])
-        if g == 1:
-            send_all(CH_Q + g, tx[CH_Q + g], rx[CH_Q + g])
+        send_all(CH_Q + g, tx[CH_Q + g], rx[CH_Q + g])
 
     whole_w[f, 0] = weight[:half]
     whole_w[f, 1] = weight[half:]
@@ -194,70 +193,80 @@
         )
         values_f32[...] = term if first else values_f32[...] + term
 
-    add_values(0, True)
-
     def forward(i):
         w_arrival(i).wait_recv()
         w_forward(i).start()
 
-    each(1, n_f, forward)
-
     def later_values(i):
         w_forwarded(i).wait_recv()
         add_values(i, False)
 
-    each(1, n_f, later_values)
-    values[...] = values_f32[...].astype(jnp.bfloat16).reshape(values.shape)
-    to_slots(values, 0, KV_COLS, send_block, tx[CH_V], rx[CH_V])
-    send_all(CH_V, tx[CH_V], rx[CH_V])
-    for g in range(2, KV_HEADS):
-        send_all(CH_Q + g, tx[CH_Q + g], rx[CH_Q + g])
-
-    recv_all(CH_K, tx[CH_K], rx[CH_K])
-    from_slots(rx[CH_K], take_from, packed_k, 0, KV_COLS)
+    def make_values():
+        add_values(0, True)
+        each(1, n_f, later_values)
+        values[...] = values_f32[...].astype(jnp.bfloat16).reshape(values.shape)
+        to_slots(values, 0, KV_COLS, send_block, tx[CH_V], rx[CH_V])
+        send_all(CH_V, tx[CH_V], rx[CH_V])
 
     scale = HEAD_DIM ** (-0.5)
 
-    def attend(g):
+    tiles = rows // TILE
+
+    def head_cols(g):
+        return [
+            slice(g * GROUP_COLS + x * HEAD_DIM, g * GROUP_COLS + (x + 1) * HEAD_DIM)
+            for x in range(GROUP)
+        ]
+
+    def stacked(ref, here, g):
+        return jnp.concatenate([ref[here, h] for h in head_cols(g)], axis=0)
+
+    def find_probs(g):
         recv_all(CH_Q + g, tx[CH_Q + g], rx[CH_Q + g])
         from_slots(rx[CH_Q + g], take_from, packed_q, g * GROUP_COLS, GROUP_COLS)
-        if g == 0:
-            recv_all(CH_V, tx[CH_V], rx[CH_V])
-            from_slots(rx[CH_V], take_from, packed_v, 0, KV_COLS)
         kv = slice(g * HEAD_DIM, (g + 1) * HEAD_DIM)
-        for t in reversed(range(rows // TILE)):
+        for t in reversed(range(tiles)):
             span = (t + 1) * TILE
             here = slice(t * TILE, span)
-            heads = [
-                slice(g * GROUP_COLS + x * HEAD_DIM, g * GROUP_COLS + (x + 1) * HEAD_DIM)
-                for x in range(GROUP)
-            ]
-            q = jnp.concatenate([packed_q[here, h] for h in heads], axis=0)
-            og = jnp.concatenate([out_grad[here, h] for h in heads], axis=0)
+            q = stacked(packed_q, here, g)
+            s = lax.dot_general(q, packed_k[:span, kv], NT, preferred_element_type=jnp.float32)
+            s = (s * scale).reshape(GROUP, TILE, span) + bias[here, :span][None]
+            s = s.reshape(GROUP * TILE, span)
+            e = jnp.exp(s - jnp.max(s, axis=-1, keepdims=True))
+            p = e * (1.0 / jnp.sum(e, axis=-1, keepdims=True))
+            probs[g, t, :, :span] = p
+            og = stacked(out_grad, here, g)
+            dv = lax.dot_general(p.astype(jnp.bfloat16), og, TN, preferred_element_type=jnp.float32)
+            if span == rows:
+                dv_acc[...] = dv
+            else:
+                dv_acc[:span] += dv
+        vg = dv_acc[...].astype(jnp.bfloat16)
+        value_grad[:, :, kv] = vg.reshape(blocks, BLOCK_ROWS, HEAD_DIM)
+
+    def find_grads(g):
+        kv = slice(g * HEAD_DIM, (g + 1) * HEAD_DIM)
+        for t in reversed(range(tiles)):
+            span = (t + 1) * TILE
+            here = slice(t * TILE, span)
+            q = stacked(packed_q, here, g)
+            og = stacked(out_grad, here, g)
             k = packed_k[:span, kv]
             v = packed_v[:span, kv]
-            s = lax.dot_general(q, k, NT, preferred_element_type=jnp.float32) * scale
-            s = (s.reshape(GROUP, TILE, span) + bias[here, :span][None]).reshape(GROUP * TILE, span)
-            peak = jnp.max(s, axis=-1, keepdims=True)
-            e = jnp.exp(s - peak)
-            p = e * (1.0 / jnp.sum(e, axis=-1, keepdims=True))
+            p = probs[g, t, :, :span]
             ph = p.astype(jnp.bfloat16)
             pg = lax.dot_general(og, v, NT, preferred_element_type=jnp.float32)
             delta = jnp.sum(ph.astype(jnp.float32) * pg, axis=-1, keepdims=True)
             ds = (p * (pg - delta) * scale).astype(jnp.bfloat16)
             dq = jnp.dot(ds, k, preferred_element_type=jnp.float32).astype(jnp.bfloat16)
-            for x, h in enumerate(heads):
+            for x, h in enumerate(head_cols(g)):
                 query_grad[here, h] = dq[x * TILE : (x + 1) * TILE]
             dk = lax.dot_general(ds, q, TN, preferred_element_type=jnp.float32)
-            dv = lax.dot_general(ph, og, TN, preferred_element_type=jnp.float32)
             if span == rows:
                 dk_acc[...] = dk
-                dv_acc[...] = dv
             else:
                 dk_acc[:span] += dk
-                dv_acc[:span] += dv
         key_grad[:, kv] = dk_acc[...].astype(jnp.bfloat16)
-        value_grad[:, :, kv] = dv_acc[...].astype(jnp.bfloat16).reshape(blocks, BLOCK_ROWS, HEAD_DIM)
 
     def return_values(h):
         to_slots(value_grad, h * HALF_COLS, HALF_COLS, take_block, gtx[h], grx[h])
@@ -367,26 +376,35 @@
             acc = acc + z_rx[h, z_peer(i)].astype(jnp.float32)
         weight_grad[:, h * HALF_COLS : (h + 1) * HALF_COLS] = acc * grad_scale
 
-    attend(0)
-    attend(1)
+    def input_cols(at):
+        w = whole_w[at].reshape(shard, KV_COLS)
+        vg = value_grad[...].reshape(rows, KV_COLS)
+        x = lax.dot_general(vg, w, NT, preferred_element_type=jnp.float32)
+        input_grad[:, pl.ds(pl.multiple_of(at * shard, 128), shard)] = x.astype(jnp.bfloat16)
+
+    recv_all(CH_K, tx[CH_K], rx[CH_K])
+    from_slots(rx[CH_K], take_from, packed_k, 0, KV_COLS)
+    find_probs(0)
+    find_probs(1)
     return_values(0)
-    attend(2)
+    each(1, n_f, forward)
+    find_probs(2)
+    make_values()
     weight_terms(0)
-    attend(3)
+    find_probs(3)
     return_values(1)
     weight_pairs(0)
-
-    def input_cols(at):
-        w = whole_w[at].reshape(shard, KV_COLS)
-        x = lax.dot_general(value_grad[...].reshape(rows, KV_COLS), w, NT, preferred_element_type=jnp.float32)
-        input_grad[:, pl.ds(pl.multiple_of(at * shard, 128), shard)] = x.astype(jnp.bfloat16)
-
+    each(0, n_f, input_cols)
     weight_terms(1)
-    each(0, n_f // 2, input_cols)
+    recv_all(CH_V, tx[CH_V], rx[CH_V])
+    from_slots(rx[CH_V], take_from, packed_v, 0, KV_COLS)
     weight_pairs(1)
     weight_squares(0)
-    each(n_f // 2, n_f, input_cols)
+    find_grads(0)
+    find_grads(1)
+    find_grads(2)
     weight_squares(1)
+    find_grads(3)
     weight_lines(0)
     weight_lines(1)
 
@@ -446,6 +464,7 @@
             pltpu.VMEM((rows, rows), jnp.float32),
             pltpu.VMEM((rows, HEAD_DIM), jnp.float32),
             pltpu.VMEM((rows, HEAD_DIM), jnp.float32),
+            pltpu.VMEM((KV_HEADS, rows // TILE, GROUP * TILE, rows), jnp.float32),
             pltpu.VMEM((rows // BLOCK_ROWS, BLOCK_ROWS, KV_COLS), half),
             pltpu.VMEM((2, rows, HALF_COLS), half),
             pltpu.VMEM((2, n_z, dest_rows, HALF_COLS), half),
@@ -459,7 +478,7 @@
             dma((2,)), dma((2,)), dma((2, n_f)), dma((2, n_f)), dma((2, n_z)), dma((2, n_z)),
         ],
         compiler_params=pltpu.CompilerParams(
-            collective_id=0, has_side_effects=True, vmem_limit_bytes=56 * 1024 * 1024
+            collective_id=0, has_side_effects=True, vmem_limit_bytes=42 * 1024 * 1024
         ),
         cost_estimate=pl.CostEstimate(
             flops=10_000_000_000, bytes_accessed=16_000_000, transcendentals=2_400_000

time: 119 us -> 111 us (0.933)
  Pallas kernels: 108 us -> 97 us
  local copies, waits for them, and re-layouts: 7.02 us -> 11.3 us
    pallas_call x1, Pallas kernels: 108 us -> 97 us  [local(): pl.pallas_call(functools.partial(kernel, n_dp, n_f, (rows * n_dp * n_f) *...]
    unnamed x8 -> x18, local copies, waits for them, and re-layouts: 7.02 us -> 11.3 us
where the time goes in v2:
time: 111 us; the launch traced here: 110 us
  Pallas kernels  97 us (87%)
  local copies, waits for them, and re-layouts  11.3 us (10%)
  other arithmetic  1.48 us (1%)
    pallas_call x1, Pallas kernels, local(): pl.pallas_call(functools.partial(kernel, n_dp, n_f, (rows * n_dp * n_f) *...  97 us
    unnamed x18, local copies, waits for them, and re-layouts  11.3 us

profile of v2, /device:TPU:0, one launch (start us, length us, event | category | flops | bytes accessed | tf_op | source)
XLA Modules:
  0.0 110.4 jit_solution(18175338029341059566)
XLA Ops:
  0.6 0.7 select_reduce_fusion
  1.4 0.7 select_reduce_fusion.1
  2.1 0.0 copy-start
  2.1 1.4 %copy-done = bf16[384,2048]{1,0:T(8,128)(2,1)S(1)} copy-done((bf16[384,2048]{1,0:T(8,128)(2,1)S(1)}, bf16[384,2048]{1,0:T(8,128)(2,1)}, u32[]{:S(2)}) %copy-start) | copy-done | bytes 1572888
  3.5 0.0 copy-start.1
  3.5 1.4 %copy-done.1 = bf16[384,2048]{1,0:T(8,128)(2,1)S(1)} copy-done((bf16[384,2048]{1,0:T(8,128)(2,1)S(1)}, bf16[384,2048]{1,0:T(8,128)(2,1)}, u32[]{:S(2)}) %copy-start.1) | copy-done | bytes 1572888
  4.9 0.0 copy-start.2
  4.9 1.2 %copy-done.2 = bf16[1024,512]{1,0:T(8,128)(2,1)S(1)} copy-done((bf16[1024,512]{1,0:T(8,128)(2,1)S(1)}, bf16[1024,512]{1,0:T(8,128)(2,1)}, u32[]{:S(2)}) %copy-start.2) | copy-done | bytes 1048600
  6.2 0.0 copy-start.3
  6.2 1.0 copy-done.3
  7.1 0.0 copy-start.4
  7.2 0.7 copy-done.4
  7.8 0.0 copy-start.5
  7.8 0.7 copy-done.5
  8.5 0.0 copy-start.6
  8.5 0.7 copy-done.6
  9.1 97.0 %packed_backward.1 = (bf16[384,2048]{1,0:T(8,128)(2,1)S(1)}, bf16[384,512]{1,0:T(8,128)(2,1)S(1)}, bf16[384,4096]{1,0:T(8,128)(2,1)S(1)}, f32[128,512]{1,0:T(8,128)S(1)}) custom-call(bf16[384,4096]{1,0:T(8,128)(2,1)} %normed.1, bf16[8,48,2048]{2,1,0:T(8,128)(2,1)S(1)} %bitcast.6, bf16[8,48,512]{2,1,0:T(8,128)(2,1)S(1)} %bitcast.7, ...), custom_call_target="tpu_custom_call" | custom-call | flops 10000000000 | bytes 16000000 | tf_op jit(solution)/shard_map/packed_backward/pallas_call | solution.py:445
  106.1 1.1 %copy.16 = bf16[384,2048]{1,0:T(8,128)(2,1)} copy(bf16[384,2048]{1,0:T(8,128)(2,1)S(1)} %get-tuple-element.8) | data formatting | bytes 3145728
  107.3 0.7 copy.17
  108.0 1.7 %copy.18 = bf16[384,4096]{1,0:T(8,128)(2,1)} copy(bf16[384,4096]{1,0:T(8,128)(2,1)S(1)} %get-tuple-element.10) | data formatting | bytes 6291456
  109.7 0.7 copy.19
Async XLA Ops:
  2.1 1.4 %copy-start = (bf16[384,2048]{1,0:T(8,128)(2,1)S(1)}, bf16[384,2048]{1,0:T(8,128)(2,1)}, u32[]{:S(2)}) copy-start(bf16[384,2048]{1,0:T(8,128)(2,1)} %param.9) | copy-start | bytes 4718596
  3.5 1.4 %copy-start.1 = (bf16[384,2048]{1,0:T(8,128)(2,1)S(1)}, bf16[384,2048]{1,0:T(8,128)(2,1)}, u32[]{:S(2)}) copy-start(bf16[384,2048]{1,0:T(8,128)(2,1)} %out_grad.1) | copy-start | bytes 4718596
  4.9 1.2 %copy-start.2 = (bf16[1024,512]{1,0:T(8,128)(2,1)S(1)}, bf16[1024,512]{1,0:T(8,128)(2,1)}, u32[]{:S(2)}) copy-start(bf16[1024,512]{1,0:T(8,128)(2,1)} %weight.1) | copy-start | bytes 3145732
  6.2 1.0 copy-start.3
  7.1 0.7 copy-start.4
  7.8 0.7 copy-start.5
  8.5 0.7 copy-start.6

commit v3 on v2

--- a/solution.py
+++ b/solution.py
@@ -25,8 +25,9 @@
 
 def kernel(
     n_dp, n_f, grad_scale,
-    normed, queries, keys, out_grad, weight, doc_row, send_to, take_from, send_block, take_block,
+    normed_in, queries_in, keys_in, out_grad_in, weight_in, doc_row, send_to, take_from, send_block, take_block,
     query_grad, key_grad, input_grad, weight_grad,
+    normed, queries, keys, out_grad, weight, in_sem,
     tx, rx, gtx, grx, whole_w, values_f32, values, packed_q, packed_k, packed_v,
     normed_t, bias, dk_acc, dv_acc, probs, value_grad, home, pair_tx, pair_rx, pair_sum,
     f_rx, z_tx, z_rx,
@@ -52,6 +53,17 @@
     def f_peer(i):
         return lax.rem(f + i, n_f)
 
+    def load(at, source, out):
+        copy = pltpu.make_async_copy(source, out, in_sem.at[at])
+        copy.start()
+        return copy
+
+    keys_load = load(0, keys_in, keys)
+    queries_load = load(1, queries_in, queries)
+    weight_load = load(2, weight_in, weight)
+    normed_load = load(3, normed_in, normed)
+    out_grad_load = load(4, out_grad_in, out_grad)
+
     barrier = pltpu.get_barrier_semaphore()
 
     def greet_dp(i, _):
@@ -156,8 +168,11 @@
             device_id_type=MESH,
         )
 
+    keys_load.wait()
     to_slots(keys, 0, KV_COLS, send_block, tx[CH_K], rx[CH_K])
+    queries_load.wait()
     to_slots(queries, 0, GROUP_COLS, send_block, tx[CH_Q], rx[CH_Q])
+    weight_load.wait()
     pl.semaphore_wait(barrier, n_dp + n_f - 2)
 
     each(1, n_f, lambda i: w_copy(i).start())
@@ -167,6 +182,8 @@
         to_slots(queries, g * GROUP_COLS, GROUP_COLS, send_block, tx[CH_Q + g], rx[CH_Q + g])
         send_all(CH_Q + g, tx[CH_Q + g], rx[CH_Q + g])
 
+    normed_load.wait()
+    out_grad_load.wait()
     whole_w[f, 0] = weight[:half]
     whole_w[f, 1] = weight[half:]
 
@@ -205,6 +222,8 @@
         add_values(0, True)
         each(1, n_f, later_values)
         values[...] = values_f32[...].astype(jnp.bfloat16).reshape(values.shape)
+
+    def send_values():
         to_slots(values, 0, KV_COLS, send_block, tx[CH_V], rx[CH_V])
         send_all(CH_V, tx[CH_V], rx[CH_V])
 
@@ -390,20 +409,22 @@
     each(1, n_f, forward)
     find_probs(2)
     make_values()
-    weight_terms(0)
     find_probs(3)
     return_values(1)
+    send_values()
+    weight_terms(0)
+    each(0, n_f // 2, input_cols)
     weight_pairs(0)
-    each(0, n_f, input_cols)
     weight_terms(1)
+    each(n_f // 2, n_f, input_cols)
+    weight_pairs(1)
+    weight_squares(0)
     recv_all(CH_V, tx[CH_V], rx[CH_V])
     from_slots(rx[CH_V], take_from, packed_v, 0, KV_COLS)
-    weight_pairs(1)
-    weight_squares(0)
     find_grads(0)
     find_grads(1)
+    weight_squares(1)
     find_grads(2)
-    weight_squares(1)
     find_grads(3)
     weight_lines(0)
     weight_lines(1)
@@ -430,6 +451,7 @@
     half = jnp.bfloat16
     vmem = pl.BlockSpec(memory_space=pltpu.VMEM)
     smem = pl.BlockSpec(memory_space=pltpu.SMEM)
+    hbm = pl.BlockSpec(memory_space=pltpu.HBM)
     dma = pltpu.SemaphoreType.DMA
     slots = [pltpu.VMEM((n_dp, BLOCK_ROWS, KV_COLS), half) for _ in range(CH_G)]
     half_slots = [pltpu.VMEM((n_dp, BLOCK_ROWS, HALF_COLS), half) for _ in range(2)]
@@ -450,9 +472,15 @@
             jax.ShapeDtypeStruct(normed.shape, half),
             jax.ShapeDtypeStruct((piece, KV_COLS), jnp.float32),
         ),
-        in_specs=[vmem] * 6 + [smem] * 4,
+        in_specs=[hbm] * 5 + [vmem] + [smem] * 4,
         out_specs=(vmem,) * 4,
         scratch_shapes=[
+            pltpu.VMEM(normed.shape, half),
+            pltpu.VMEM((blocks, BLOCK_ROWS, queries.shape[1]), half),
+            pltpu.VMEM((blocks, BLOCK_ROWS, key_rows.shape[1]), half),
+            pltpu.VMEM(out_grad.shape, half),
+            pltpu.VMEM(value_weight.shape, half),
+            dma((5,)),
             list(slots), list(slots), list(half_slots), list(half_slots),
             pltpu.VMEM((n_f, 2, shard // 2, KV_COLS), half),
             pltpu.VMEM((rows, KV_COLS), jnp.float32),
@@ -478,7 +506,7 @@
             dma((2,)), dma((2,)), dma((2, n_f)), dma((2, n_f)), dma((2, n_z)), dma((2, n_z)),
         ],
         compiler_params=pltpu.CompilerParams(
-            collective_id=0, has_side_effects=True, vmem_limit_bytes=42 * 1024 * 1024
+            collective_id=0, has_side_effects=True, vmem_limit_bytes=53 * 1024 * 1024
         ),
         cost_estimate=pl.CostEstimate(
             flops=10_000_000_000, bytes_accessed=16_000_000, transcendentals=2_400_000

time: 111 us -> 104 us (0.937)
  Pallas kernels: 97 us -> 93.5 us
  local copies, waits for them, and re-layouts: 11.3 us -> 7.98 us
    pallas_call x1, Pallas kernels: 97 us -> 93.5 us  [local(): pl.pallas_call(functools.partial(kernel, n_dp, n_f, (rows * n_dp * n_f) *...]
    unnamed x18 -> x12, local copies, waits for them, and re-layouts: 11.3 us -> 7.98 us
where the time goes in v3:
time: 104 us
  Pallas kernels  93.5 us (90%)
  local copies, waits for them, and re-layouts  7.98 us (8%)
  other arithmetic  1.48 us (1%)
    pallas_call x1, Pallas kernels, local(): pl.pallas_call(functools.partial(kernel, n_dp, n_f, (rows * n_dp * n_f) *...  93.5 us
    unnamed x12, local copies, waits for them, and re-layouts  7.98 us

profile of v3, /device:TPU:0, one launch (start us, length us, event | category | flops | bytes accessed | tf_op | source)
XLA Modules:
  0.0 103.6 jit_solution(2285147362309959760)
XLA Ops:
  0.6 0.7 select_reduce_fusion
  1.4 0.7 select_reduce_fusion.1
  2.1 0.0 copy-start
  2.1 0.7 copy-done
  2.8 0.0 copy-start.1
  2.8 0.7 copy-done.1
  3.4 0.0 copy-start.2
  3.4 0.7 copy-done.2
  4.1 93.5 %packed_backward.1 = (bf16[384,2048]{1,0:T(8,128)(2,1)}, bf16[384,512]{1,0:T(8,128)(2,1)S(1)}, bf16[384,4096]{1,0:T(8,128)(2,1)}, f32[128,512]{1,0:T(8,128)S(1)}) custom-call(bf16[384,4096]{1,0:T(8,128)(2,1)} %normed_in.1, bf16[8,48,2048]{2,1,0:T(8,128)(2,1)} %bitcast.10, bf16[8,48,512]{2,1,0:T(8,128)(2,1)} %bitcast.11, bf16[384,2048]{1,0:T(8,128)(2,1)} %out_grad_in.1, ...), custom_call_target="tpu_custom_call" | custom-call | flops 10000000000 | bytes 16000000 | tf_op jit(solution)/shard_map/packed_backward/pallas_call | solution.py:467
  97.6 0.0 copy-start.3
  97.6 2.9 %copy.16 = bf16[384,2048]{1,0:T(8,128)(2,1)} copy(bf16[384,2048]{1,0:T(8,128)(2,1)} %get-tuple-element.8) | data formatting | bytes 3145728
  100.5 0.7 copy.17
  101.2 0.0 copy-done.3
  101.2 1.7 %copy.18 = bf16[384,4096]{1,0:T(8,128)(2,1)} copy(bf16[384,4096]{1,0:T(8,128)(2,1)S(1)} %copy-done.3) | data formatting | bytes 6291456
  102.9 0.7 copy.19
Async XLA Ops:
  2.1 0.7 copy-start
  2.8 0.7 copy-start.1
  3.4 0.7 copy-start.2
  97.6 3.6 %copy-start.3 = (bf16[384,4096]{1,0:T(8,128)(2,1)S(1)}, bf16[384,4096]{1,0:T(8,128)(2,1)}, u32[]{:S(2)}) copy-start(bf16[384,4096]{1,0:T(8,128)(2,1)} %get-tuple-element.10) | copy-start | bytes 9437188
